TPU v7x, 256 devices: a whole 4x4x8 slice. The times are simulated.
256 devices in a mesh: group: 8 (over y, core), member: 32 (over z, x).
Axes of the slice: x: 4, y: 4, z: 8, core: 2. Of those that a mesh axis runs over, the one named last changes fastest.
Arguments:
- right_side: float32 [4096, 64, 128], P(('group', 'member')), may hold values from -70 to 70
- a_diagonal: float32 [4096, 128], P(('group', 'member')), may hold values from 1.05 to 3
- a_tiles: float32 [4096, 5, 128, 128], P(('group', 'member')), may hold values from 0 to 0.0333333333
- a_columns: int32 [4096, 5], P(('group', 'member')), may hold values from 0 to 23, as said below
- g_diagonal: float32 [4096, 128], P(('group', 'member')), may hold values from 0.5 to 2
- g_tiles: float32 [4096, 4, 128, 128], P(('group', 'member')), may hold values from 0 to 0.03125
- g_columns: int32 [4096, 4], P(('group', 'member')), may hold values from 0 to 23, as said below
- owned_counts: int32 [256], P(('group', 'member')), may hold values from 8 to 16, as said below
- send_lists: int32 [256, 4, 2], P(('group', 'member')), may hold values from 0 to 15
Outputs:
- solution: float32 [4096, 64, 128], P(('group', 'member'))
- residual: float32 [4096, 64, 128], P(('group', 'member'))
Inputs may be any that keep to these rules, and one draw needn't show every extreme that they name: Block rows from owned_counts of a device up to 15 are padding; some device holds exactly 16 live block rows and some exactly 8. `a_columns`: indices into the device's extended list; for a fixed tile position k no index appears twice among one device's block rows. `g_columns`: indices into the device's extended list; for a fixed tile position k no index appears twice among one device's block rows.
All inputs are finite; a program needn't handle non-finite values.
Results may differ from a plain program's by a relative error of at most 0.0003.
Values sent between devices are 32-bit elements; how exact they have to be, the bound alone decides.
No kernel may reach another device: no remote copies, remote signals or barrier semaphores. Data moves between devices by JAX's collectives and lax.ppermute only.
A program may use at most 64 MiB of HBM per device.

v0:
```python
import jax
import jax.numpy as jnp
from jax import lax
from jax.sharding import PartitionSpec as P

ITERS = 3


PRECISE = lax.Precision.HIGHEST


def extended_2(value, sides, width):
    for axis, dim in sides:
        peers, length = (lax.axis_size(axis), value.shape[dim])
        up = [(i, (i + 1) % peers) for i in range(peers - 1)]
        down = [(j, i) for i, j in up]
        last = lax.slice_in_dim(value, length - width, length, axis=dim)
        initial = lax.slice_in_dim(value, 0, width, axis=dim)
        before = lax.ppermute(last, axis, up)
        after = lax.ppermute(initial, axis, down)
        value = jnp.concatenate([before, value, after], axis=dim)
    return value


def neighbour_blocks(vector, outgoing):
    packed_member = jnp.stack(
        [jnp.take(vector, outgoing[1], axis=0), jnp.take(vector, outgoing[0], axis=0)]
    )
    wide_member = extended_2(packed_member, (("member", 0),), 1)
    packed_group = jnp.stack(
        [jnp.take(vector, outgoing[3], axis=0), jnp.take(vector, outgoing[2], axis=0)]
    )
    wide_group = extended_2(packed_group, (("group", 0),), 1)
    below_member, above_member = (wide_member[0], wide_member[3])
    below_group, above_group = (wide_group[0], wide_group[3])
    return jnp.concatenate([vector, below_member, above_member, below_group, above_group], axis=0)


def row_products(tile_set, column_ids, extended):
    picked = jnp.take(extended, column_ids.reshape(-1), axis=0)
    picked = picked.reshape(column_ids.shape + extended.shape[1:])
    return jnp.einsum("rkij,rknj->rni", tile_set, picked, precision=PRECISE)


def column_sums(tile_set, column_ids, vector, outgoing):
    blocks_here = vector.shape[0]
    slot_count = outgoing.shape[1]
    extent = blocks_here + 4 * slot_count
    contrib = jnp.einsum("rkij,rni->rknj", tile_set, vector, precision=PRECISE)
    flattened = contrib.reshape((-1,) + vector.shape[1:])
    onehot = (column_ids.reshape(-1)[:, None] == jnp.arange(extent)[None, :]).astype(jnp.float32)
    sums_wide = jnp.einsum("te,tnb->enb", onehot, flattened, precision=PRECISE)
    own_rows = sums_wide[:blocks_here]
    pieces = [
        sums_wide[blocks_here + facing * slot_count : blocks_here + (facing + 1) * slot_count]
        for facing in range(4)
    ]
    back_member = extended_2(jnp.stack([pieces[0], pieces[1]]), (("member", 0),), 1)
    back_group = extended_2(jnp.stack([pieces[2], pieces[3]]), (("group", 0),), 1)
    arrivals = jnp.concatenate(
        [back_member[3], back_member[0], back_group[3], back_group[0]], axis=0
    )
    targets = outgoing.reshape(-1)
    onehot_back = (targets[:, None] == jnp.arange(blocks_here)[None, :]).astype(jnp.float32)
    return own_rows + jnp.einsum("sr,snb->rnb", onehot_back, arrivals, precision=PRECISE)


def inner(first_vec, second_vec):
    return jnp.sum(first_vec * second_vec, axis=(0, 2))


def on_device(
    right_side,
    a_diagonal,
    a_tiles,
    a_columns,
    g_diagonal,
    g_tiles,
    g_columns,
    owned_counts,
    send_lists,
):
    outgoing = send_lists[0]
    blocks_here = right_side.shape[0]
    live_rows = (jnp.arange(blocks_here) < owned_counts[0]).astype(jnp.float32)[:, None, None]
    a_scale = a_diagonal[:, None, :]
    g_scale = g_diagonal[:, None, :]

    def apply_factors(vector):
        forward = row_products(g_tiles, g_columns, neighbour_blocks(vector, outgoing))
        halfway = (g_scale * vector + forward) * live_rows
        return (g_scale * halfway + column_sums(g_tiles, g_columns, halfway, outgoing)) * live_rows

    residual = right_side * live_rows
    solution = jnp.zeros_like(residual)

    def global_sum(values):
        return lax.psum(values, ("group", "member"))

    preconditioned = apply_factors(residual)
    rho_now = global_sum(inner(residual, preconditioned))
    direction = preconditioned
    for iteration in range(ITERS):
        lower_part = row_products(a_tiles, a_columns, neighbour_blocks(direction, outgoing))
        upper_part = column_sums(a_tiles, a_columns, direction, outgoing)
        pressure_image = (a_scale * direction - lower_part - upper_part) * live_rows
        step_size = rho_now / global_sum(inner(direction, pressure_image))
        solution = solution + step_size[:, None] * direction
        residual = residual - step_size[:, None] * pressure_image
        if iteration + 1 < ITERS:
            preconditioned = apply_factors(residual)
            rho_next = global_sum(inner(residual, preconditioned))
            direction = preconditioned + (rho_next / rho_now)[:, None] * direction
            rho_now = rho_next
    return (solution, residual)


def solution(mesh):
    return jax.shard_map(
        on_device,
        mesh=mesh,
        in_specs=(
            P(("group", "member"), None, None),
            P(("group", "member"), None),
            P(("group", "member"), None, None, None),
            P(("group", "member"), None),
            P(("group", "member"), None),
            P(("group", "member"), None, None, None),
            P(("group", "member"), None),
            P(("group", "member")),
            P(("group", "member"), None, None),
        ),
        out_specs=(P(("group", "member"), None, None), P(("group", "member"), None, None)),
        check_vma=False,
    )
```

profile of v0, /device:TPU:1, one launch (start us, length us, event | category | flops | bytes accessed | tf_op | source)
XLA Modules:
  0.0 736.7 jit_solution(12116200544370071778)
XLA Ops:
  4.2 3.9 collective-permute-start
  10.9 4.0 collective-permute-start.2
  18.2 3.0 collective-permute-done.3
  21.1 2.0 gather_fusion.4
  26.0 4.5 fusion.20
  30.5 2.4 fusion.43
  36.9 2.4 collective-permute-start.6
  39.3 4.3 collective-permute-start.5
  45.4 4.1 collective-permute-done.4
  50.4 3.5 fusion.41
  53.9 2.4 fusion.4
  58.8 3.7 collective-permute-start.15
  64.4 3.1 collective-permute-start.13
  68.9 5.5 collective-permute-start.8
  77.1 6.0 collective-permute-done.9
  83.1 5.5 collective-permute-start.10
  91.9 4.3 collective-permute-done.11
  96.1 2.2 gather_fusion.9
  98.4 2.0 broadcast_select_fusion.2
  100.9 8.5 %multiply_reduce_fusion.4 = (f32[64]{0:T(128)S(1)}, f32[64]{0:T(128)S(1)}, f32[16,64,128]{2,1,0:T(8,128)S(1)}) fusion(f32[16,64,128]{2,1,0:T(8,128)S(1)} %get-tuple-element.26, f32[16,64,128]{2,1,0:T(8,128)S(1)} %get-tuple-element.28, f32[16]{0:T(128)S(1)} %compare_convert_fusion, f32[16,64,128]{2,0,1:T(8,128)S(1)} %fusion.53, ...), kind=kOutput, calls=%fused_computation.103 | convolution fusion | flops 1007812480 | bytes 10494528 | tf_op jit(solution)/shard_map/rkij,rknj->rni/dot_general | solution.py:42
  109.5 87.9 %all-reduce = (f32[64]{0:T(128)S(1)}, f32[64]{0:T(128)S(1)}) all-reduce(f32[64]{0:T(128)S(1)} %get-tuple-element.6, f32[64]{0:T(128)S(1)} %get-tuple-element.4), channel_id=1, replica_groups=mesh['group'=8,'member'=32] {'group','member'}, use_global_device_ids=true, to_apply=%region_1.4 | all-reduce | flops 128 | bytes 1024 | tf_op jit(solution)/shard_map/psum | solution.py:98
  199.9 2.3 collective-permute-start.16
  205.7 2.3 collective-permute-start.19
  208.1 3.2 collective-permute-done.19
  211.3 2.0 gather_fusion.14
  216.1 4.4 fusion.17
  220.6 2.4 fusion.39
  227.0 2.4 collective-permute-start.22
  229.4 4.5 collective-permute-start.21
  235.7 4.2 collective-permute-done.20
  240.9 82.5 %psum.44 = f32[64]{0:T(128)S(1)} all-reduce(f32[64]{0:T(128)S(1)} %get-tuple-element.21), channel_id=1, replica_groups=mesh['group'=8,'member'=32] {'group','member'}, use_global_device_ids=true, to_apply=%region_5.9 | all-reduce | flops 64 | bytes 512 | tf_op jit(solution)/shard_map/psum | solution.py:98
  323.6 5.1 fusion.37
  328.8 2.4 fusion.2
  334.2 3.6 collective-permute-start.31
  339.8 3.1 collective-permute-start.29
  344.3 4.0 collective-permute-start.24
  351.1 4.4 collective-permute-done.25
  355.6 4.4 collective-permute-start.26
  363.3 4.3 collective-permute-done.27
  367.6 2.2 gather_fusion.19
  373.2 8.5 %multiply_reduce_fusion.2 = (f32[64]{0:T(128)S(1)}, f32[16,64,128]{2,1,0:T(8,128)S(1)}) fusion(f32[16,64,128]{2,1,0:T(8,128)S(1)} %get-tuple-element.20, f32[16]{0:T(128)S(1)} %compare_convert_fusion, f32[16,64,128]{2,0,1:T(8,128)S(1)} %fusion.69, f32[16,64,128]{2,0,1:T(8,128)S(1)} %slice.235, f32[16,5,64,128]{3,2,1,0:T(8,128)S(1)} %bitcast.315, ...), kind=kOutput, calls=%fused_computation.99 | convolution fusion | flops 1007550400 | bytes 9969984 | tf_op jit(solution)/shard_map/rkij,rknj->rni/dot_general | solution.py:42
  381.8 81.7 %psum.45 = f32[64]{0:T(128)S(1)} all-reduce(f32[64]{0:T(128)S(1)} %get-tuple-element.56), channel_id=1, replica_groups=mesh['group'=8,'member'=32] {'group','member'}, use_global_device_ids=true, to_apply=%region_7.11 | all-reduce | flops 64 | bytes 512 | tf_op jit(solution)/shard_map/psum | solution.py:98
  466.0 3.1 collective-permute-start.32
  472.6 2.6 collective-permute-start.35
  475.3 2.9 collective-permute-done.35
  478.2 2.0 gather_fusion.24
  483.0 4.4 fusion.14
  487.5 2.4 fusion.35
  493.9 2.4 collective-permute-start.38
  496.4 4.5 collective-permute-start.37
  502.7 4.2 collective-permute-done.36
  507.9 82.6 %psum.46 = f32[64]{0:T(128)S(1)} all-reduce(f32[64]{0:T(128)S(1)} %get-tuple-element.15), channel_id=1, replica_groups=mesh['group'=8,'member'=32] {'group','member'}, use_global_device_ids=true, to_apply=%region_9.13 | all-reduce | flops 64 | bytes 512 | tf_op jit(solution)/shard_map/psum | solution.py:98
  590.7 5.1 fusion.33
  595.8 2.4 fusion
  602.8 3.6 collective-permute-start.47
  608.3 3.1 collective-permute-start.45
  613.7 4.0 collective-permute-start.40
  621.3 3.7 collective-permute-done.41
  625.0 4.5 collective-permute-start.42
  632.8 4.3 collective-permute-done.43
  637.1 2.3 gather_fusion.29
  642.9 9.2 %multiply_reduce_fusion = (f32[64]{0:T(128)S(1)}, f32[16,64,128]{2,1,0:T(8,128)}) fusion(f32[16,64,128]{2,1,0:T(8,128)S(1)} %get-tuple-element.14, f32[16]{0:T(128)S(1)} %compare_convert_fusion, f32[16,64,128]{2,0,1:T(8,128)S(1)} %fusion.85, f32[16,64,128]{2,0,1:T(8,128)S(1)} %slice.245, f32[16,5,64,128]{3,2,1,0:T(8,128)S(1)} %bitcast.313, ...), kind=kOutput, calls=%fused_computation.95 | convolution fusion | flops 1007550400 | bytes 9969984 | tf_op jit(solution)/shard_map/rkij,rknj->rni/dot_general | solution.py:42
  652.1 81.9 %psum.47 = f32[64]{0:T(128)S(1)} all-reduce(f32[64]{0:T(128)S(1)} %get-tuple-element.58), channel_id=1, replica_groups=mesh['group'=8,'member'=32] {'group','member'}, use_global_device_ids=true, to_apply=%region_11.15 | all-reduce | flops 64 | bytes 512 | tf_op jit(solution)/shard_map/psum | solution.py:98
  734.0 2.3 multiply_subtract_fusion
  (250 shorter events, 96.2 us)
Async XLA Ops:
  0.6 17.1 %copy-start.5 = (s32[1,4,2]{1,2,0:T(2,128)S(1)}, s32[1,4,2]{1,2,0:T(2,128)}, u32[]{:S(2)}) copy-start(s32[1,4,2]{1,2,0:T(2,128)} %param.23) | copy-start | bytes 100
  0.7 17.1 %copy-start.15 = (s32[16,5]{0,1:T(8,128)S(1)}, s32[16,5]{0,1:T(8,128)}, u32[]{:S(2)}) copy-start(s32[16,5]{0,1:T(8,128)} %param.18) | copy-start | bytes 964
  1.7 464.2 %copy-start.6 = (pred[2]{0:T(512)(128)(4,1)}, pred[2]{0:T(512)(128)(4,1)S(1)}, u32[]{:S(2)}) copy-start(pred[2]{0:T(512)(128)(4,1)S(1)} %compare_and_fusion.5) | copy-start | bytes 10
  4.2 13.9 %collective-permute-start = (f32[1,2,64,128]{3,2,1,0:T(8,128)S(1)}, f32[1,2,64,128]{3,2,1,0:T(8,128)S(1)}, u32[]{:S(2)}, u32[]{:S(2)}) collective-permute-start(f32[1,2,64,128]{3,2,1,0:T(8,128)S(1)} %select_bitcast_fusion.23), channel_id=1, source_target_pairs={{0,1},{1,2},{2,3},{3,4},{4,5},{5,6},{6,7},{7,8},{8,9},{9,10},{10,1... | collective-permute-start | bytes 196616 | tf_op jit(solution)/shard_map/ppermute | solution.py:19
  8.2 461.0 %copy-start.7 = (pred[2]{0:T(512)(128)(4,1)}, pred[2]{0:T(512)(128)(4,1)S(1)}, u32[]{:S(2)}) copy-start(pred[2]{0:T(512)(128)(4,1)S(1)} %compare_and_fusion.4) | copy-start | bytes 10
  8.9 9.3 %collective-permute-start.1 = (f32[1,2,64,128]{3,2,1,0:T(8,128)S(1)}, f32[1,2,64,128]{3,2,1,0:T(8,128)S(1)}, u32[]{:S(2)}, u32[]{:S(2)}) collective-permute-start(f32[1,2,64,128]{3,2,1,0:T(8,128)S(1)} %select_bitcast_fusion.22), channel_id=1, source_target_pairs={{1,0},{2,1},{3,2},{4,3},{5,4},{6,5},{7,6},{8,7},{9,8},{10,9},{11,1... | collective-permute-start | bytes 196616 | tf_op jit(solution)/shard_map/ppermute | solution.py:20
  10.2 460.4 %copy-start.8 = (pred[2]{0:T(512)(128)(4,1)}, pred[2]{0:T(512)(128)(4,1)S(1)}, u32[]{:S(2)}) copy-start(pred[2]{0:T(512)(128)(4,1)S(1)} %compare_and_fusion.3) | copy-start | bytes 10
  10.2 454.6 %copy-start.11 = (s32[1024]{0:T(1024)}, s32[1024]{0:T(1024)S(1)}, u32[]{:S(2)}) copy-start(s32[1024]{0:T(1024)S(1)} %get-tuple-element.61) | copy-start | bytes 12292
  10.2 455.2 %copy-start.10 = (s32[1024]{0:T(1024)}, s32[1024]{0:T(1024)S(1)}, u32[]{:S(2)}) copy-start(s32[1024]{0:T(1024)S(1)} %get-tuple-element.60) | copy-start | bytes 12292
  10.9 7.3 collective-permute-start.2
  14.9 457.6 %copy-start.9 = (pred[2]{0:T(512)(128)(4,1)}, pred[2]{0:T(512)(128)(4,1)S(1)}, u32[]{:S(2)}) copy-start(pred[2]{0:T(512)(128)(4,1)S(1)} %compare_and_fusion.2) | copy-start | bytes 10
  15.6 5.6 collective-permute-start.3
  18.0 351.8 %copy-start.13 = (pred[80]{0:T(512)(128)(4,1)}, pred[80]{0:T(512)(128)(4,1)S(1)}, u32[]{:S(2)}) copy-start(pred[80]{0:T(512)(128)(4,1)S(1)} %compare_and_fusion) | copy-start | bytes 244
  30.4 19.9 %slice-start = ((s8[5242880]{0:T(1024)(128)(4,1)}), s8[4194304]{0:T(1024)(128)(4,1)S(1)}, s32[]{:S(2)}) async-start(s8[5242880]{0:T(1024)(128)(4,1)} %bitcast.308), calls=%async_computation | async-start | bytes 8388608
  32.9 17.5 %slice-start.1 = ((s8[5242880]{0:T(1024)(128)(4,1)}), s8[1048576]{0:T(1024)(128)(4,1)S(1)}, s32[]{:S(2)}) async-start(s8[5242880]{0:T(1024)(128)(4,1)} %bitcast.308), calls=%async_computation.1 | async-start | bytes 2097152
  35.0 10.2 %collective-permute-start.7 = (f32[1,2,64,128]{3,1,2,0:T(2,128)S(1)}, f32[1,2,64,128]{3,1,2,0:T(2,128)S(1)}, u32[]{:S(2)}, u32[]{:S(2)}) collective-permute-start(f32[1,2,64,128]{3,1,2,0:T(2,128)S(1)} %get-tuple-element.50), channel_id=1, source_target_pairs={{0,32},{32,64},{64,96},{96,128},{128,160},{160,192},{192,224},{1,3... | collective-permute-start | bytes 196616 | tf_op jit(solution)/shard_map/ppermute | solution.py:19
  36.9 8.3 %collective-permute-start.6 = (f32[1,2,64,128]{3,1,2,0:T(2,128)S(1)}, f32[1,2,64,128]{3,1,2,0:T(2,128)S(1)}, u32[]{:S(2)}, u32[]{:S(2)}) collective-permute-start(f32[1,2,64,128]{3,1,2,0:T(2,128)S(1)} %get-tuple-element.51), channel_id=1, source_target_pairs={{32,0},{64,32},{96,64},{128,96},{160,128},{192,160},{224,192},{33,... | collective-permute-start | bytes 196616 | tf_op jit(solution)/shard_map/ppermute | solution.py:20
  39.3 6.1 collective-permute-start.5
  43.6 5.9 collective-permute-start.4
  45.1 322.4 %copy-start.12 = (s32[1024]{0:T(1024)}, s32[1024]{0:T(1024)S(1)}, u32[]{:S(2)}) copy-start(s32[1024]{0:T(1024)S(1)} %pad_clamp_fusion) | copy-start | bytes 12292
  58.8 41.6 %collective-permute-start.15 = (f32[1,2,64,128]{3,1,2,0:T(2,128)S(1)}, f32[1,2,64,128]{3,1,2,0:T(2,128)S(1)}, u32[]{:S(2)}, u32[]{:S(2)}) collective-permute-start(f32[1,2,64,128]{3,1,2,0:T(2,128)S(1)} %get-tuple-element.46), channel_id=1, source_target_pairs={{0,32},{32,64},{64,96},{96,128},{128,160},{160,192},{192,224},{1,3... | collective-permute-start | bytes 196616 | tf_op jit(solution)/shard_map/ppermute | solution.py:19
  62.5 37.9 %collective-permute-start.14 = (f32[1,2,64,128]{3,1,2,0:T(2,128)S(1)}, f32[1,2,64,128]{3,1,2,0:T(2,128)S(1)}, u32[]{:S(2)}, u32[]{:S(2)}) collective-permute-start(f32[1,2,64,128]{3,1,2,0:T(2,128)S(1)} %get-tuple-element.47), channel_id=1, source_target_pairs={{32,0},{64,32},{96,64},{128,96},{160,128},{192,160},{224,192},{33,... | collective-permute-start | bytes 196616 | tf_op jit(solution)/shard_map/ppermute | solution.py:20
  64.4 36.0 %collective-permute-start.13 = (f32[1,2,64,128]{3,1,2,0:T(2,128)S(1)}, f32[1,2,64,128]{3,1,2,0:T(2,128)S(1)}, u32[]{:S(2)}, u32[]{:S(2)}) collective-permute-start(f32[1,2,64,128]{3,1,2,0:T(2,128)S(1)} %get-tuple-element.48), channel_id=1, source_target_pairs={{0,1},{1,2},{2,3},{3,4},{4,5},{5,6},{6,7},{7,8},{8,9},{9,10},{10,1... | collective-permute-start | bytes 196616 | tf_op jit(solution)/shard_map/ppermute | solution.py:19
  67.5 32.8 %collective-permute-start.12 = (f32[1,2,64,128]{3,1,2,0:T(2,128)S(1)}, f32[1,2,64,128]{3,1,2,0:T(2,128)S(1)}, u32[]{:S(2)}, u32[]{:S(2)}) collective-permute-start(f32[1,2,64,128]{3,1,2,0:T(2,128)S(1)} %get-tuple-element.45), channel_id=1, source_target_pairs={{1,0},{2,1},{3,2},{4,3},{5,4},{6,5},{7,6},{8,7},{9,8},{10,9},{11,1... | collective-permute-start | bytes 196616 | tf_op jit(solution)/shard_map/ppermute | solution.py:20
  68.9 6.9 collective-permute-start.8
  75.8 7.3 collective-permute-start.9
  83.1 6.9 collective-permute-start.10
  89.9 6.2 collective-permute-start.11
  199.9 8.2 %collective-permute-start.16 = (f32[1,2,64,128]{3,2,1,0:T(8,128)S(1)}, f32[1,2,64,128]{3,2,1,0:T(8,128)S(1)}, u32[]{:S(2)}, u32[]{:S(2)}) collective-permute-start(f32[1,2,64,128]{3,2,1,0:T(8,128)S(1)} %select_bitcast_fusion.15), channel_id=1, source_target_pairs={{0,1},{1,2},{2,3},{3,4},{4,5},{5,6},{6,7},{7,8},{8,9},{9,10},{10,1... | collective-permute-start | bytes 196616 | tf_op jit(solution)/shard_map/ppermute | solution.py:19
  202.3 5.8 collective-permute-start.17
  203.6 4.5 collective-permute-start.18
  205.7 5.6 collective-permute-start.19
  225.1 10.2 %collective-permute-start.23 = (f32[1,2,64,128]{3,1,2,0:T(2,128)S(1)}, f32[1,2,64,128]{3,1,2,0:T(2,128)S(1)}, u32[]{:S(2)}, u32[]{:S(2)}) collective-permute-start(f32[1,2,64,128]{3,1,2,0:T(2,128)S(1)} %get-tuple-element.42), channel_id=1, source_target_pairs={{0,32},{32,64},{64,96},{96,128},{128,160},{160,192},{192,224},{1,3... | collective-permute-start | bytes 196616 | tf_op jit(solution)/shard_map/ppermute | solution.py:19
  227.0 8.2 %collective-permute-start.22 = (f32[1,2,64,128]{3,1,2,0:T(2,128)S(1)}, f32[1,2,64,128]{3,1,2,0:T(2,128)S(1)}, u32[]{:S(2)}, u32[]{:S(2)}) collective-permute-start(f32[1,2,64,128]{3,1,2,0:T(2,128)S(1)} %get-tuple-element.43), channel_id=1, source_target_pairs={{32,0},{64,32},{96,64},{128,96},{160,128},{192,160},{224,192},{33,... | collective-permute-start | bytes 196616 | tf_op jit(solution)/shard_map/ppermute | solution.py:20
  229.4 6.3 collective-permute-start.21
  233.9 6.0 collective-permute-start.20
  334.2 37.5 %collective-permute-start.31 = (f32[1,2,64,128]{3,1,2,0:T(2,128)}, f32[1,2,64,128]{3,1,2,0:T(2,128)}, u32[]{:S(2)}, u32[]{:S(2)}) collective-permute-start(f32[1,2,64,128]{3,1,2,0:T(2,128)} %get-tuple-element.38), channel_id=1, source_target_pairs={{0,32},{32,64},{64,96},{96,128},{128,160},{160,192},{192,224},{1,3... | collective-permute-start | bytes 196616 | tf_op jit(solution)/shard_map/ppermute | solution.py:19
  337.9 33.9 %collective-permute-start.30 = (f32[1,2,64,128]{3,1,2,0:T(2,128)}, f32[1,2,64,128]{3,1,2,0:T(2,128)}, u32[]{:S(2)}, u32[]{:S(2)}) collective-permute-start(f32[1,2,64,128]{3,1,2,0:T(2,128)} %get-tuple-element.39), channel_id=1, source_target_pairs={{32,0},{64,32},{96,64},{128,96},{160,128},{192,160},{224,192},{33,... | collective-permute-start | bytes 196616 | tf_op jit(solution)/shard_map/ppermute | solution.py:20
  339.8 32.0 %collective-permute-start.29 = (f32[1,2,64,128]{3,1,2,0:T(2,128)S(1)}, f32[1,2,64,128]{3,1,2,0:T(2,128)}, u32[]{:S(2)}, u32[]{:S(2)}) collective-permute-start(f32[1,2,64,128]{3,1,2,0:T(2,128)S(1)} %get-tuple-element.40), channel_id=1, source_target_pairs={{0,1},{1,2},{2,3},{3,4},{4,5},{5,6},{6,7},{7,8},{8,9},{9,10},{10,1... | collective-permute-start | bytes 196616 | tf_op jit(solution)/shard_map/ppermute | solution.py:19
  342.9 28.9 %collective-permute-start.28 = (f32[1,2,64,128]{3,1,2,0:T(2,128)S(1)}, f32[1,2,64,128]{3,1,2,0:T(2,128)}, u32[]{:S(2)}, u32[]{:S(2)}) collective-permute-start(f32[1,2,64,128]{3,1,2,0:T(2,128)S(1)} %get-tuple-element.37), channel_id=1, source_target_pairs={{1,0},{2,1},{3,2},{4,3},{5,4},{6,5},{7,6},{8,7},{9,8},{10,9},{11,1... | collective-permute-start | bytes 196616 | tf_op jit(solution)/shard_map/ppermute | solution.py:20
  344.3 5.6 collective-permute-start.24
  349.8 5.7 collective-permute-start.25
  355.6 5.8 collective-permute-start.26
  361.3 6.2 collective-permute-start.27
  373.2 90.2 %copy-start.22 = (f32[64]{0:T(128)S(1)}, f32[64]{0:T(128)}, u32[]{:S(2)}) copy-start(f32[64]{0:T(128)} %copy-done.21) | copy-start | bytes 772
  466.0 9.2 %collective-permute-start.32 = (f32[1,2,64,128]{3,2,1,0:T(8,128)S(1)}, f32[1,2,64,128]{3,2,1,0:T(8,128)S(1)}, u32[]{:S(2)}, u32[]{:S(2)}) collective-permute-start(f32[1,2,64,128]{3,2,1,0:T(8,128)S(1)} %select_bitcast_fusion.7), channel_id=1, source_target_pairs={{0,1},{1,2},{2,3},{3,4},{4,5},{5,6},{6,7},{7,8},{8,9},{9,10},{10,1... | collective-permute-start | bytes 196616 | tf_op jit(solution)/shard_map/ppermute | solution.py:19
  469.2 6.0 collective-permute-start.33
  470.6 4.7 collective-permute-start.34
  472.6 5.6 collective-permute-start.35
  492.0 10.2 %collective-permute-start.39 = (f32[1,2,64,128]{3,1,2,0:T(2,128)S(1)}, f32[1,2,64,128]{3,1,2,0:T(2,128)S(1)}, u32[]{:S(2)}, u32[]{:S(2)}) collective-permute-start(f32[1,2,64,128]{3,1,2,0:T(2,128)S(1)} %get-tuple-element.34), channel_id=1, source_target_pairs={{0,32},{32,64},{64,96},{96,128},{128,160},{160,192},{192,224},{1,3... | collective-permute-start | bytes 196616 | tf_op jit(solution)/shard_map/ppermute | solution.py:19
  493.9 8.3 %collective-permute-start.38 = (f32[1,2,64,128]{3,1,2,0:T(2,128)S(1)}, f32[1,2,64,128]{3,1,2,0:T(2,128)S(1)}, u32[]{:S(2)}, u32[]{:S(2)}) collective-permute-start(f32[1,2,64,128]{3,1,2,0:T(2,128)S(1)} %get-tuple-element.35), channel_id=1, source_target_pairs={{32,0},{64,32},{96,64},{128,96},{160,128},{192,160},{224,192},{33,... | collective-permute-start | bytes 196616 | tf_op jit(solution)/shard_map/ppermute | solution.py:20
  496.4 6.3 collective-permute-start.37
  500.9 6.0 collective-permute-start.36
  602.8 38.6 %collective-permute-start.47 = (f32[1,2,64,128]{3,1,2,0:T(2,128)}, f32[1,2,64,128]{3,1,2,0:T(2,128)}, u32[]{:S(2)}, u32[]{:S(2)}) collective-permute-start(f32[1,2,64,128]{3,1,2,0:T(2,128)} %get-tuple-element.30), channel_id=1, source_target_pairs={{0,32},{32,64},{64,96},{96,128},{128,160},{160,192},{192,224},{1,3... | collective-permute-start | bytes 196616 | tf_op jit(solution)/shard_map/ppermute | solution.py:19
  606.4 35.0 %collective-permute-start.46 = (f32[1,2,64,128]{3,1,2,0:T(2,128)}, f32[1,2,64,128]{3,1,2,0:T(2,128)}, u32[]{:S(2)}, u32[]{:S(2)}) collective-permute-start(f32[1,2,64,128]{3,1,2,0:T(2,128)} %get-tuple-element.31), channel_id=1, source_target_pairs={{32,0},{64,32},{96,64},{128,96},{160,128},{192,160},{224,192},{33,... | collective-permute-start | bytes 196616 | tf_op jit(solution)/shard_map/ppermute | solution.py:20
  608.3 33.1 %collective-permute-start.45 = (f32[1,2,64,128]{3,1,2,0:T(2,128)}, f32[1,2,64,128]{3,1,2,0:T(2,128)}, u32[]{:S(2)}, u32[]{:S(2)}) collective-permute-start(f32[1,2,64,128]{3,1,2,0:T(2,128)} %get-tuple-element.32), channel_id=1, source_target_pairs={{0,1},{1,2},{2,3},{3,4},{4,5},{5,6},{6,7},{7,8},{8,9},{9,10},{10,1... | collective-permute-start | bytes 196616 | tf_op jit(solution)/shard_map/ppermute | solution.py:19
  611.4 30.0 %collective-permute-start.44 = (f32[1,2,64,128]{3,1,2,0:T(2,128)}, f32[1,2,64,128]{3,1,2,0:T(2,128)}, u32[]{:S(2)}, u32[]{:S(2)}) collective-permute-start(f32[1,2,64,128]{3,1,2,0:T(2,128)} %get-tuple-element.29), channel_id=1, source_target_pairs={{1,0},{2,1},{3,2},{4,3},{5,4},{6,5},{7,6},{8,7},{9,8},{10,9},{11,1... | collective-permute-start | bytes 196616 | tf_op jit(solution)/shard_map/ppermute | solution.py:20
  613.7 6.3 collective-permute-start.40
  620.0 5.0 collective-permute-start.41
  625.0 5.8 collective-permute-start.42
  630.9 6.2 collective-permute-start.43
  642.9 91.1 %copy-start.24 = (f32[64]{0:T(128)S(1)}, f32[64]{0:T(128)}, u32[]{:S(2)}) copy-start(f32[64]{0:T(128)} %copy-done.23) | copy-start | bytes 772
  642.9 91.1 %copy-start.17 = (f32[64]{0:T(128)S(1)}, f32[64]{0:T(128)}, u32[]{:S(2)}) copy-start(f32[64]{0:T(128)} %copy-done.16) | copy-start | bytes 772
  642.9 91.1 %copy-start.19 = (f32[64]{0:T(128)S(1)}, f32[64]{0:T(128)}, u32[]{:S(2)}) copy-start(f32[64]{0:T(128)} %copy-done.18) | copy-start | bytes 772
  (11 other events, 67.9 us)
where the time goes:
time: 746 us; the launch traced here: 737 us
  blocking collectives  417 us (56%)
  starting transfers between devices  126 us (17%)
  matrix products  78.8 us (11%)
  waiting for transfers between devices  55.8 us (7%)
  local copies, waits for them, and re-layouts  34 us (5%)
  other arithmetic  22.4 us (3%)
    psum x5, blocking collectives, global_sum(): return lax.psum(values, ('group', 'member'))  417 us
    ppermute x24, starting transfers between devices, extended_2(): before = lax.ppermute(last, axis, up)  84.6 us
    ppermute x24, waiting for transfers between devices, extended_2(): after = lax.ppermute(initial, axis, down)  48.4 us
    ppermute x24, starting transfers between devices, extended_2(): after = lax.ppermute(initial, axis, down)  41.2 us
    dot_general x6, matrix products, row_products(): return jnp.einsum('rkij,rknj->rni', tile_set, picked, precision=PRECISE)  39.6 us
    dot_general x6, matrix products, column_sums(): contrib = jnp.einsum('rkij,rni->rknj', tile_set, vector, precision=PRECISE)  21.1 us
  transfers between devices with their start and end apart: 48, of which 20 were waited for; matrix products, arithmetic and copies ran while one was open for 3% of the time, Pallas kernels for 0%

commit v1 on v0

v1 whole, which is shorter than its diff:
```python
import functools

import jax
import jax.numpy as jnp
from jax import lax
from jax.experimental import pallas as pl
from jax.experimental.pallas import tpu as pltpu
from jax.sharding import PartitionSpec as P

SHIFT = 4.0
LISTS = 4
f32 = jnp.float32
bf16 = jnp.bfloat16
VMEM = pl.BlockSpec(memory_space=pltpu.VMEM)
SMEM = pl.BlockSpec(memory_space=pltpu.SMEM)


def halves(x):
    high = x.astype(bf16)
    low = (x - high.astype(f32)).astype(bf16)
    return high, low


def stacked(x):
    return jnp.concatenate(halves(x), axis=0)


def beside(x):
    return jnp.concatenate(halves(x), axis=1)


def product(rows, tile):
    out = jnp.dot(rows, tile, preferred_element_type=f32)
    n, m = out.shape[0] // 2, out.shape[1] // 2
    out = out[:n] + out[n:]
    return out[:, :m] + out[:, m:]


class Meta:
    def __init__(self, ref, tiles):
        self.ref = ref
        self.tiles = tiles

    def column(self, b, k):
        return self.ref[b * self.tiles + k]

    def sent(self, i, s):
        return self.ref[16 * self.tiles + 2 * i + s]

    def live(self, b):
        return b < self.ref[16 * self.tiles + 8]

    def valid(self, i):
        return self.ref[16 * self.tiles + 9 + i] > 0


def assemble(meta, part, msgs, recvs, ext):
    for b in range(16):
        ext[b] = part[b]
    for i in range(LISTS):
        valid = meta.valid(i)
        for s in range(2):
            row = meta.sent(i ^ 1, s)
            ext[row] += jnp.where(valid, recvs[i][2 + s], 0.0)
            ext[16 + 2 * i + s] = jnp.where(valid, recvs[i][s] + msgs[i ^ 1][2 + s], 0.0)


def fill_messages(meta, part, sums, sign, msgs):
    for i in range(LISTS):
        for s in range(2):
            msgs[i][s] = part[meta.sent(i, s)]
            msgs[i][2 + s] = sign * sums[16 + 2 * (i ^ 1) + s]


def forward_row(meta, b, tile_ref, split_ref):
    picked = []
    turned = []
    for k in range(meta.tiles):
        picked.append(split_ref[meta.column(b, k)])
        turned.append(beside(tile_ref[b, k].T))
    return product(jnp.concatenate(picked, axis=1), jnp.concatenate(turned, axis=0))


def transposed_row(meta, b, tile_ref, rows, sums):
    for k in range(meta.tiles):
        sums[meta.column(b, k)] += product(rows, beside(tile_ref[b, k]))


def pack_kernel(meta_ref, right_ref, m0, m1, m2, m3):
    meta = Meta(meta_ref, 4)
    for i, msg in enumerate((m0, m1, m2, m3)):
        for s in range(2):
            msg[s] = right_ref[meta.sent(i, s)]


def factor_kernel(first, meta_ref, diag_ref, tile_ref, *refs):
    meta = Meta(meta_ref, 4)
    if first:
        right_ref, r0, r1, r2, r3 = refs[:5]
        recvs = (r0, r1, r2, r3)
        own_ref, half_ref, part_ref, m0, m1, m2, m3, ext, split_ref, sums = refs[5:]
        for b in range(16):
            ext[b] = jnp.where(meta.live(b), right_ref[b], 0.0)
        for i in range(LISTS):
            for s in range(2):
                ext[16 + 2 * i + s] = jnp.where(meta.valid(i), recvs[i][s], 0.0)
    else:
        part_in = refs[0]
        own_ref, half_ref, part_ref, m0, m1, m2, m3, ext, split_ref, sums = refs[9:]
        assemble(meta, part_in, refs[1:5], refs[5:9], ext)
    for m in range(24):
        split_ref[m] = stacked(ext[m])
    sums[...] = jnp.zeros_like(sums)
    for b in range(16):
        own_ref[b] = ext[b]
    for b in range(16):
        forward = forward_row(meta, b, tile_ref, split_ref)
        half = jnp.where(meta.live(b), diag_ref[b : b + 1] * ext[b] + forward, 0.0)
        half_ref[b] = half
        transposed_row(meta, b, tile_ref, stacked(half), sums)
    for b in range(16):
        part_ref[b] = jnp.where(meta.live(b), diag_ref[b : b + 1] * half_ref[b] + sums[b], 0.0)
    fill_messages(meta, part_ref, sums, 1.0, (m0, m1, m2, m3))


def pressure_kernel(last, meta_ref, diag_ref, tile_ref, *refs):
    meta = Meta(meta_ref, 5)
    part_in, msgs, recvs = refs[0], refs[1:5], refs[5:9]
    if last:
        gram_ref = refs[9]
        own_ref, part_ref, m0, m1, m2, m3, pay_ref, ext, split_ref, sums = refs[10:]
    else:
        basis_ref = refs[9]
        own_ref, part_ref, m0, m1, m2, m3, ext, split_ref, sums = refs[10:]
    assemble(meta, part_in, msgs, recvs, ext)
    for m in range(24):
        split_ref[m] = stacked(ext[m])
    sums[...] = jnp.zeros_like(sums)
    for b in range(16):
        own_ref[b] = ext[b]
    energy = jnp.zeros(ext.shape[1:], f32)
    for b in range(16):
        forward = forward_row(meta, b, tile_ref, split_ref)
        scaled = diag_ref[b : b + 1] * ext[b]
        part_ref[b] = scaled - forward
        if last:
            energy = energy + ext[b] * (scaled - 2.0 * forward)
        transposed_row(meta, b, tile_ref, split_ref[b], sums)
    for b in range(16):
        value = part_ref[b] - sums[b]
        if not last:
            value = value - SHIFT * basis_ref[b]
        part_ref[b] = jnp.where(meta.live(b), value, 0.0)
    fill_messages(meta, part_ref, sums, -1.0, (m0, m1, m2, m3))
    if last:
        place = lax.broadcasted_iota(jnp.int32, energy.shape, 1)
        table = gram_ref[...] + jnp.where(place == 6, jnp.sum(energy, axis=1, keepdims=True), 0.0)
        turned = jnp.concatenate([table, jnp.zeros_like(table)], axis=0).T[:8]
        for i in range(8):
            pay_ref[i] = turned


def gram_kernel(y0, y1, y2, out_ref):
    pairs = ((y0, y0), (y0, y1), (y0, y2), (y1, y1), (y1, y2), (y2, y2))
    totals = [jnp.zeros(out_ref.shape, f32) for _ in pairs]
    for b in range(16):
        totals = [total + left[b] * right[b] for total, (left, right) in zip(totals, pairs)]
    place = lax.broadcasted_iota(jnp.int32, out_ref.shape, 1)
    table = jnp.zeros(out_ref.shape, f32)
    for i, total in enumerate(totals):
        table = table + jnp.where(place == i, jnp.sum(total, axis=1, keepdims=True), 0.0)
    out_ref[...] = table


def cg_scalars(g):
    gram = {(0, 0): g[0], (0, 1): g[1], (0, 2): g[2], (1, 1): g[3], (1, 2): g[4], (2, 2): g[5]}
    energy = {(2, 2): g[6]}
    for i in range(2):
        for j in range(i, 3):
            energy[i, j] = gram[min(i + 1, j), max(i + 1, j)] + SHIFT * gram[i, j]

    def form(table, c):
        total = 0.0
        for i in range(len(c)):
            for j in range(i, len(c)):
                term = c[i] * c[j] * table[i, j]
                total = total + (term if i == j else 2.0 * term)
        return total

    zero = jnp.zeros_like(g[0])
    one = jnp.ones_like(g[0])
    x = [zero, zero, zero]
    r = [one, zero, zero, zero]
    p = [one]
    rho = gram[0, 0]
    for step in range(3):
        alpha = rho / form(energy, p)
        for i, c in enumerate(p):
            x[i] = x[i] + alpha * c
            r[i] = r[i] - SHIFT * (alpha * c)
            r[i + 1] = r[i + 1] - alpha * c
        if step < 2:
            rho_next = form(gram, r[: step + 2])
            beta = rho_next / rho
            p = [r[i] + beta * (p[i] if i < len(p) else 0.0) for i in range(step + 2)]
            rho = rho_next
    return x + r


def final_kernel(meta_ref, sums_ref, v0, v1, v2, w0, w1, w2, part_ref, r0, r1, r2, r3, x_ref, res_ref, w3):
    meta = Meta(meta_ref, 5)
    total = sums_ref[0]
    for i in range(1, sums_ref.shape[0]):
        total = total + sums_ref[i]
    rows = cg_scalars([total[i : i + 1] for i in range(7)])
    rows = jnp.concatenate(rows + [jnp.zeros((121, 128), f32)], axis=0)
    columns = rows.T[:64]
    c = [jnp.broadcast_to(columns[:, i : i + 1], (64, 128)) for i in range(7)]
    for b in range(16):
        w3[b] = part_ref[b]
    for i, recv in enumerate((r0, r1, r2, r3)):
        for s in range(2):
            w3[meta.sent(i ^ 1, s)] += jnp.where(meta.valid(i), recv[2 + s], 0.0)
    for b in range(16):
        x_ref[b] = c[0] * v0[b] + c[1] * v1[b] + c[2] * v2[b]
        res_ref[b] = c[3] * w0[b] + c[4] * w1[b] + (c[5] - SHIFT * c[6]) * w2[b] + c[6] * w3[b]


def call(kernel, outs, scratch=(), smem=1):
    def run(*args):
        return pl.pallas_call(
            kernel,
            out_shape=tuple(jax.ShapeDtypeStruct(shape, f32) for shape in outs),
            in_specs=[SMEM] * smem + [VMEM] * (len(args) - smem),
            out_specs=(VMEM,) * len(outs),
            scratch_shapes=list(scratch),
            compiler_params=pltpu.CompilerParams(vmem_limit_bytes=32 * 2**20),
        )(*args)

    return run


def on_device(
    right_side,
    a_diagonal,
    a_tiles,
    a_columns,
    g_diagonal,
    g_tiles,
    g_columns,
    owned_counts,
    send_lists,
):
    groups, members = lax.axis_size("group"), lax.axis_size("member")
    group, member = lax.axis_index("group"), lax.axis_index("member")
    valid = jnp.stack([member > 0, member < members - 1, group > 0, group < groups - 1])
    tail = [send_lists.reshape(-1), owned_counts, valid.astype(jnp.int32)]
    a_meta = jnp.concatenate([a_columns.reshape(-1)] + tail)
    g_meta = jnp.concatenate([g_columns.reshape(-1)] + tail)

    own = (16, 64, 128)
    message = (4, 64, 128)

    def exchange(msgs):
        out = []
        for msg, axis, size, way in zip(
            msgs, ("member", "member", "group", "group"), (members, members, groups, groups), (1, -1, 1, -1)
        ):
            out.append(lax.ppermute(msg, axis, [(i, (i + way) % size) for i in range(size)]))
        return out

    scratch = [pltpu.VMEM((24, 64, 128), f32), pltpu.VMEM((24, 128, 128), bf16), pltpu.VMEM((24, 64, 128), f32)]
    msgs = call(pack_kernel, [(2, 64, 128)] * 4)(g_meta, right_side)
    recvs = exchange(msgs)
    basis_w, basis_v, halves_y = [], [], []
    for k in range(3):
        if k == 0:
            operands = (right_side, *recvs)
        else:
            operands = (part, *msgs, *recvs)
        w, y, part, *msgs = call(functools.partial(factor_kernel, k == 0), [own] * 3 + [message] * 4, scratch)(
            g_meta, g_diagonal, g_tiles, *operands
        )
        recvs = exchange(msgs)
        basis_w.append(w)
        halves_y.append(y)
        if k < 2:
            extra = w
            outs = [own, own] + [message] * 4
        else:
            (extra,) = call(gram_kernel, [(64, 128)], smem=0)(*halves_y)
            outs = [own, own] + [message] * 4 + [(groups, 8, 128)]
        v, part, *msgs = call(functools.partial(pressure_kernel, k == 2), outs, scratch)(
            a_meta, a_diagonal, a_tiles, part, *msgs, *recvs, extra
        )
        basis_v.append(v)
        if k == 2:
            *msgs, payload = msgs
        recvs = exchange(msgs)
    sums = jnp.sum(lax.all_to_all(payload, "group", 0, 0), axis=0)
    sums = lax.all_to_all(jnp.broadcast_to(sums[None], (members, 8, 128)), "member", 0, 0)
    return call(final_kernel, [own, own], [pltpu.VMEM(own, f32)])(
        a_meta, sums, *basis_v, *basis_w, part, *recvs
    )


def solution(mesh):
    return jax.shard_map(
        on_device,
        mesh=mesh,
        in_specs=(
            P(("group", "member"), None, None),
            P(("group", "member"), None),
            P(("group", "member"), None, None, None),
            P(("group", "member"), None),
            P(("group", "member"), None),
            P(("group", "member"), None, None, None),
            P(("group", "member"), None),
            P(("group", "member")),
            P(("group", "member"), None, None),
        ),
        out_specs=(P(("group", "member"), None, None), P(("group", "member"), None, None)),
        check_vma=False,
    )
```

time: 746 us -> 152 us (0.20); the launches traced: 737 us -> 151 us
  blocking collectives: 417 us -> 13.3 us
  matrix products: 78.8 us -> 0 us
  starting transfers between devices: 126 us -> 63.7 us
  waiting for transfers between devices: 55.8 us -> 15.4 us
  Pallas kernels: 0 us -> 28.1 us
  other arithmetic: 22.4 us -> 2.02 us
    psum x5 -> x0, blocking collectives: 417 us -> none  [global_sum(): return lax.psum(values, ('group', 'member'))]
    dot_general x24 -> x0, matrix products: 78.8 us -> none  [the longest x6 39.6 us: row_products(): return jnp.einsum('rkij,rknj->rni', tile_set, picked, precision=PRECISE)]
    ppermute x48 -> x28, starting transfers between devices: 126 us -> 57.9 us  [exchange(): lax.ppermute(msg, axis, [(i, (i + way) % size) for i in range(size)])]
    ppermute x48 -> x28, waiting for transfers between devices: 55.8 us -> 15.4 us  [exchange(): lax.ppermute(msg, axis, [(i, (i + way) % size) for i in range(size)])]
    pallas_call x0 -> x9, Pallas kernels: none -> 28.1 us  [run(): pl.pallas_call(kernel, out_shape=tuple((jax.ShapeDtypeStruct(shape, f32)...]
    gather x30 -> x0, local copies, waits for them, and re-layouts: 27.6 us -> none  [the longest x6 12.8 us: row_products(): picked = jnp.take(extended, column_ids.reshape(-1), axis=0)]
    unnamed x75 -> x65, local copies, waits for them, and re-layouts: 3.08 us -> 25.1 us
    all_to_all x0 -> x1, blocking collectives: none -> 13.3 us  [on_device(): sums = jnp.sum(lax.all_to_all(payload, 'group', 0, 0), axis=0)]
  transfers between devices with their start and end apart: 48 -> 29, of which waited for: 20 -> 12; matrix products, arithmetic and copies ran while one was open for 3% -> 2% of each run, Pallas kernels for 0% -> 0%
where the time goes in v1:
time: 152 us; the launch traced here: 151 us
  starting transfers between devices  63.7 us (42%)
  Pallas kernels  28.1 us (18%)
  local copies, waits for them, and re-layouts  27.2 us (18%)
  waiting for transfers between devices  15.4 us (10%)
  blocking collectives  13.3 us (9%)
  other arithmetic  2.02 us (1%)
  between operations  1.53 us (1%)
    ppermute x28, starting transfers between devices, exchange(): lax.ppermute(msg, axis, [(i, (i + way) % size) for i in range(size)])  57.9 us
    pallas_call x9, Pallas kernels, run(): pl.pallas_call(kernel, out_shape=tuple((jax.ShapeDtypeStruct(shape, f32)...  28.1 us
    unnamed x65, local copies, waits for them, and re-layouts  25.1 us
    ppermute x28, waiting for transfers between devices, exchange(): lax.ppermute(msg, axis, [(i, (i + way) % size) for i in range(size)])  15.4 us
    all_to_all x1, blocking collectives, on_device(): sums = jnp.sum(lax.all_to_all(payload, 'group', 0, 0), axis=0)  13.3 us
    all_to_all x1, starting transfers between devices, on_device(): lax.all_to_all(jnp.broadcast_to(sums[None], (members, 8, 128)), 'member',...  5.79 us
  transfers between devices with their start and end apart: 29, of which 12 were waited for; matrix products, arithmetic and copies ran while one was open for 2% of the time, Pallas kernels for 0%

profile of v1, /device:TPU:1, one launch (start us, length us, event | category | flops | bytes accessed | tf_op | source)
XLA Modules:
  0.0 151.4 jit_solution(16112970580785149614)
XLA Ops:
  1.3 0.8 copy.15
  2.2 0.8 copy.16
  3.0 0.6 add_convert_fusion
  3.6 0.7 pad_add_fusion.1.meta_ref
  4.3 1.0 copy-done.3
  5.9 2.1 %collective-permute-start = (f32[2,64,128]{2,1,0:T(8,128)S(1)}, f32[2,64,128]{2,1,0:T(8,128)S(1)}, u32[]{:S(2)}, u32[]{:S(2)}) collective-permute-start(f32[2,64,128]{2,1,0:T(8,128)S(1)} %get-tuple-element.46), channel_id=1, source_target_pairs={{0,1},{1,2},{2,3},{3,4},{4,5},{5,6},{6,7},{7,8},{8,9},{9,10},{10,1... | collective-permute-start | bytes 196616 | tf_op jit(solution)/shard_map/ppermute | solution.py:269
  8.0 6.6 %collective-permute-start.1 = (f32[2,64,128]{2,1,0:T(8,128)S(1)}, f32[2,64,128]{2,1,0:T(8,128)S(1)}, u32[]{:S(2)}, u32[]{:S(2)}) collective-permute-start(f32[2,64,128]{2,1,0:T(8,128)S(1)} %get-tuple-element.47), channel_id=1, source_target_pairs={{0,31},{1,0},{2,1},{3,2},{4,3},{5,4},{6,5},{7,6},{8,7},{9,8},{10,9... | collective-permute-start | bytes 196616 | tf_op jit(solution)/shard_map/ppermute | solution.py:269
  14.6 2.1 %collective-permute-start.2 = (f32[2,64,128]{2,1,0:T(8,128)S(1)}, f32[2,64,128]{2,1,0:T(8,128)S(1)}, u32[]{:S(2)}, u32[]{:S(2)}) collective-permute-start(f32[2,64,128]{2,1,0:T(8,128)S(1)} %get-tuple-element.48), channel_id=1, source_target_pairs={{0,32},{32,64},{64,96},{96,128},{128,160},{160,192},{192,224},{224... | collective-permute-start | bytes 196616 | tf_op jit(solution)/shard_map/ppermute | solution.py:269
  16.8 1.3 collective-permute-done.2.refs_3_
  18.1 2.4 %collective-permute-done.3.refs_4_ = f32[2,64,128]{2,1,0:T(8,128)S(1)} collective-permute-done((f32[2,64,128]{2,1,0:T(8,128)S(1)}, f32[2,64,128]{2,1,0:T(8,128)S(1)}, u32[]{:S(2)}, u32[]{:S(2)}) %collective-permute-start.3) | collective-permute-done | bytes 65568 | tf_op jit(solution)/shard_map/ppermute | solution.py:269
  20.5 2.2 %copy-done.1 = f32[16,4,128,128]{3,2,1,0:T(8,128)S(1)} copy-done((f32[16,4,128,128]{3,2,1,0:T(8,128)S(1)}, f32[16,4,128,128]{3,2,1,0:T(8,128)}, u32[]{:S(2)}) %copy-start.1) | copy-done | bytes 4194328
  22.7 0.7 copy-done.20
  23.4 4.8 %shard_map.105 = (f32[16,64,128]{2,1,0:T(8,128)S(1)}, f32[16,64,128]{2,1,0:T(8,128)S(1)}, f32[16,64,128]{2,1,0:T(8,128)S(1)}, f32[4,64,128]{2,1,0:T(8,128)S(1)},...) custom-call(s32[77]{0:T(128)S(1)} %pad_add_fusion.1.meta_ref, ...), custom_call_target="tpu_custom_call" | custom-call | tf_op jit(solution)/shard_map/pallas_call | solution.py:231
  28.3 4.8 %collective-permute-start.5 = (f32[4,64,128]{2,1,0:T(8,128)S(1)}, f32[4,64,128]{2,1,0:T(8,128)S(1)}, u32[]{:S(2)}, u32[]{:S(2)}) collective-permute-start(f32[4,64,128]{2,1,0:T(8,128)S(1)} %get-tuple-element.52.refs_2_), channel_id=1, source_target_pairs={{0,31},{1,0},{2,1},{3,2},{4,3},{5,4},{6,5},{7,6},{8,7},{9,8},{10,9... | collective-permute-start | bytes 393224 | tf_op jit(solution)/shard_map/ppermute | solution.py:269
  33.7 0.7 copy-done.12
  34.3 1.4 copy.14
  35.7 1.3 reshape.14
  37.0 0.7 pad_add_fusion.meta_ref
  37.7 0.7 copy-done.14
  38.4 0.6 copy-done.16
  39.0 0.7 copy-done.18
  39.7 2.5 %copy-done = f32[16,5,128,128]{3,2,1,0:T(8,128)S(1)} copy-done((f32[16,5,128,128]{3,2,1,0:T(8,128)S(1)}, f32[16,5,128,128]{3,2,1,0:T(8,128)}, u32[]{:S(2)}) %copy-start) | copy-done | bytes 5242904
  42.2 0.9 copy-done.13
  43.1 0.9 copy-done.15
  44.0 0.9 copy-done.17
  44.9 0.9 copy-done.19
  45.8 4.0 %shard_map.106 = (f32[16,64,128]{2,1,0:T(8,128)S(1)}, f32[16,64,128]{2,1,0:T(8,128)S(1)}, f32[4,64,128]{2,1,0:T(8,128)S(1)}, f32[4,64,128]{2,1,0:T(8,128)S(1)}, ...) custom-call(s32[93]{0:T(128)S(1)} %pad_add_fusion.meta_ref, f32[16,128]{1,0:T(8,128)S(1)} %copy-done.22, ...), custom_call_target="tpu_custom_call" | custom-call | tf_op jit(solution)/shard_map/pallas_call | solution.py:231
  49.9 4.8 %collective-permute-start.9 = (f32[4,64,128]{2,1,0:T(8,128)S(1)}, f32[4,64,128]{2,1,0:T(8,128)S(1)}, u32[]{:S(2)}, u32[]{:S(2)}) collective-permute-start(f32[4,64,128]{2,1,0:T(8,128)S(1)} %get-tuple-element.58.refs_2_), channel_id=1, source_target_pairs={{0,31},{1,0},{2,1},{3,2},{4,3},{5,4},{6,5},{7,6},{8,7},{9,8},{10,9... | collective-permute-start | bytes 393224 | tf_op jit(solution)/shard_map/ppermute | solution.py:269
  54.6 2.3 %collective-permute-start.10 = (f32[4,64,128]{2,1,0:T(8,128)S(1)}, f32[4,64,128]{2,1,0:T(8,128)S(1)}, u32[]{:S(2)}, u32[]{:S(2)}) collective-permute-start(f32[4,64,128]{2,1,0:T(8,128)S(1)} %get-tuple-element.59.refs_3_), channel_id=1, source_target_pairs={{0,32},{32,64},{64,96},{96,128},{128,160},{160,192},{192,224},{224... | collective-permute-start | bytes 393224 | tf_op jit(solution)/shard_map/ppermute | solution.py:269
  56.9 1.2 collective-permute-start.11
  58.2 0.8 collective-permute-done.10.refs_7_
  59.0 2.3 %collective-permute-done.11.refs_8_ = f32[4,64,128]{2,1,0:T(8,128)S(1)} collective-permute-done((f32[4,64,128]{2,1,0:T(8,128)S(1)}, f32[4,64,128]{2,1,0:T(8,128)S(1)}, u32[]{:S(2)}, u32[]{:S(2)}) %collective-permute-start.11) | collective-permute-done | bytes 131104 | tf_op jit(solution)/shard_map/ppermute | solution.py:269
  61.3 2.2 %copy-done.2 = f32[16,4,128,128]{3,2,1,0:T(8,128)S(1)} copy-done((f32[16,4,128,128]{3,2,1,0:T(8,128)S(1)}, f32[16,4,128,128]{3,2,1,0:T(8,128)}, u32[]{:S(2)}) %copy-start.2) | copy-done | bytes 4194328
  63.5 4.8 %shard_map.107 = (f32[16,64,128]{2,1,0:T(8,128)S(1)}, f32[16,64,128]{2,1,0:T(8,128)S(1)}, f32[16,64,128]{2,1,0:T(8,128)S(1)}, f32[4,64,128]{2,1,0:T(8,128)S(1)},...) custom-call(s32[77]{0:T(128)S(1)} %copy-done.26, f32[16,128]{1,0:T(8,128)S(1)} %copy-done.21, ...), custom_call_target="tpu_custom_call" | custom-call | tf_op jit(solution)/shard_map/pallas_call | solution.py:231
  68.4 4.8 %collective-permute-start.13 = (f32[4,64,128]{2,1,0:T(8,128)S(1)}, f32[4,64,128]{2,1,0:T(8,128)S(1)}, u32[]{:S(2)}, u32[]{:S(2)}) collective-permute-start(f32[4,64,128]{2,1,0:T(8,128)S(1)} %get-tuple-element.63.refs_2_), channel_id=1, source_target_pairs={{0,31},{1,0},{2,1},{3,2},{4,3},{5,4},{6,5},{7,6},{8,7},{9,8},{10,9... | collective-permute-start | bytes 393224 | tf_op jit(solution)/shard_map/ppermute | solution.py:269
  73.8 2.4 %collective-permute-start.15 = (f32[4,64,128]{2,1,0:T(8,128)S(1)}, f32[4,64,128]{2,1,0:T(8,128)S(1)}, u32[]{:S(2)}, u32[]{:S(2)}) collective-permute-start(f32[4,64,128]{2,1,0:T(8,128)S(1)} %get-tuple-element.65.refs_4_), channel_id=1, source_target_pairs={{0,224},{32,0},{64,32},{96,64},{128,96},{160,128},{192,160},{224,1... | collective-permute-start | bytes 393224 | tf_op jit(solution)/shard_map/ppermute | solution.py:269
  76.2 0.8 collective-permute-done.14.refs_7_
  77.1 1.4 collective-permute-done.15.refs_8_
  78.5 3.3 %shard_map.108 = (f32[16,64,128]{2,1,0:T(8,128)S(1)}, f32[16,64,128]{2,1,0:T(8,128)S(1)}, f32[4,64,128]{2,1,0:T(8,128)S(1)}, f32[4,64,128]{2,1,0:T(8,128)S(1)}, ...) custom-call(s32[93]{0:T(128)S(1)} %pad_add_fusion.meta_ref, f32[16,128]{1,0:T(8,128)S(1)} %copy-done.22, ...), custom_call_target="tpu_custom_call" | custom-call | tf_op jit(solution)/shard_map/pallas_call | solution.py:231
  81.8 0.8 copy-done.4
  82.6 4.8 %collective-permute-start.17 = (f32[4,64,128]{2,1,0:T(8,128)S(1)}, f32[4,64,128]{2,1,0:T(8,128)S(1)}, u32[]{:S(2)}, u32[]{:S(2)}) collective-permute-start(f32[4,64,128]{2,1,0:T(8,128)S(1)} %get-tuple-element.69.refs_2_), channel_id=1, source_target_pairs={{0,31},{1,0},{2,1},{3,2},{4,3},{5,4},{6,5},{7,6},{8,7},{9,8},{10,9... | collective-permute-start | bytes 393224 | tf_op jit(solution)/shard_map/ppermute | solution.py:269
  87.7 3.7 %collective-permute-start.19 = (f32[4,64,128]{2,1,0:T(8,128)S(1)}, f32[4,64,128]{2,1,0:T(8,128)S(1)}, u32[]{:S(2)}, u32[]{:S(2)}) collective-permute-start(f32[4,64,128]{2,1,0:T(8,128)S(1)} %get-tuple-element.71.refs_4_), channel_id=1, source_target_pairs={{0,224},{32,0},{64,32},{96,64},{128,96},{160,128},{192,160},{224,1... | collective-permute-start | bytes 393224 | tf_op jit(solution)/shard_map/ppermute | solution.py:269
  91.4 0.8 collective-permute-done.18.refs_7_
  92.4 4.8 %shard_map.109 = (f32[16,64,128]{2,1,0:T(8,128)S(1)}, f32[16,64,128]{2,1,0:T(8,128)S(1)}, f32[16,64,128]{2,1,0:T(8,128)S(1)}, f32[4,64,128]{2,1,0:T(8,128)S(1)},...) custom-call(s32[77]{0:T(128)S(1)} %copy-done.26, f32[16,128]{1,0:T(8,128)S(1)} %copy-done.21, ...), custom_call_target="tpu_custom_call" | custom-call | tf_op jit(solution)/shard_map/pallas_call | solution.py:231
  97.3 4.8 %collective-permute-start.21 = (f32[4,64,128]{2,1,0:T(8,128)S(1)}, f32[4,64,128]{2,1,0:T(8,128)S(1)}, u32[]{:S(2)}, u32[]{:S(2)}) collective-permute-start(f32[4,64,128]{2,1,0:T(8,128)S(1)} %get-tuple-element.74.refs_2_), channel_id=1, source_target_pairs={{0,31},{1,0},{2,1},{3,2},{4,3},{5,4},{6,5},{7,6},{8,7},{9,8},{10,9... | collective-permute-start | bytes 393224 | tf_op jit(solution)/shard_map/ppermute | solution.py:269
  102.4 4.9 %collective-permute-start.23 = (f32[4,64,128]{2,1,0:T(8,128)S(1)}, f32[4,64,128]{2,1,0:T(8,128)S(1)}, u32[]{:S(2)}, u32[]{:S(2)}) collective-permute-start(f32[4,64,128]{2,1,0:T(8,128)S(1)} %get-tuple-element.76.refs_4_), channel_id=1, source_target_pairs={{0,224},{32,0},{64,32},{96,64},{128,96},{160,128},{192,160},{224,1... | collective-permute-start | bytes 393224 | tf_op jit(solution)/shard_map/ppermute | solution.py:269
  108.2 3.3 %shard_map.111 = (f32[16,64,128]{2,1,0:T(8,128)S(1)}, f32[16,64,128]{2,1,0:T(8,128)S(1)}, f32[4,64,128]{2,1,0:T(8,128)S(1)}, f32[4,64,128]{2,1,0:T(8,128)S(1)}, ...) custom-call(s32[93]{0:T(128)S(1)} %pad_add_fusion.meta_ref, ...), custom_call_target="tpu_custom_call" | custom-call | tf_op jit(solution)/shard_map/pallas_call | solution.py:231
  111.5 0.8 copy-done.8
  112.3 0.8 copy-done.10
  113.1 0.6 copy-done.23
  113.7 0.6 copy-done.27
  114.3 13.3 %all_to_all.10 = f32[8,8,128]{2,1,0:T(8,128)S(1)} all-to-all(f32[8,8,128]{2,1,0:T(8,128)S(1)} %get-tuple-element.80), channel_id=1, replica_groups=mesh['group'=8,'member'=32] {'group'}, dimensions={0} | all-to-all | bytes 65536 | tf_op jit(solution)/shard_map/all_to_all | solution.py:300
  127.7 0.7 broadcast_in_dim.2
  128.4 5.8 %all-to-all-start.1 = ((f32[32,8,128]{2,1,0:T(8,128)}), f32[32,8,128]{2,1,0:T(8,128)S(1)}, u32[]{:S(2)}, u32[]{:S(2)}) async-start(f32[32,8,128]{2,1,0:T(8,128)} %broadcast_in_dim.2), calls=%async_computation.1 | async-start | bytes 262144 | tf_op jit(solution)/shard_map/all_to_all | solution.py:301
  134.2 1.3 collective-permute-start.24
  135.5 3.6 %collective-permute-start.25 = (f32[4,64,128]{2,1,0:T(8,128)S(1)}, f32[4,64,128]{2,1,0:T(8,128)S(1)}, u32[]{:S(2)}, u32[]{:S(2)}) collective-permute-start(f32[4,64,128]{2,1,0:T(8,128)S(1)} %get-tuple-element.87), channel_id=1, source_target_pairs={{0,31},{1,0},{2,1},{3,2},{4,3},{5,4},{6,5},{7,6},{8,7},{9,8},{10,9... | collective-permute-start | bytes 393224 | tf_op jit(solution)/shard_map/ppermute | solution.py:269
  139.0 1.7 %collective-permute-start.26 = (f32[4,64,128]{2,1,0:T(8,128)S(1)}, f32[4,64,128]{2,1,0:T(8,128)S(1)}, u32[]{:S(2)}, u32[]{:S(2)}) collective-permute-start(f32[4,64,128]{2,1,0:T(8,128)S(1)} %get-tuple-element.88), channel_id=1, source_target_pairs={{0,32},{32,64},{64,96},{96,128},{128,160},{160,192},{192,224},{224... | collective-permute-start | bytes 393224 | tf_op jit(solution)/shard_map/ppermute | solution.py:269
  140.8 3.6 %collective-permute-done.24.r0 = f32[4,64,128]{2,1,0:T(8,128)S(1)} collective-permute-done((f32[4,64,128]{2,1,0:T(8,128)}, f32[4,64,128]{2,1,0:T(8,128)S(1)}, u32[]{:S(2)}, u32[]{:S(2)}) %collective-permute-start.24) | collective-permute-done | bytes 131104 | tf_op jit(solution)/shard_map/ppermute | solution.py:269
  144.4 1.0 collective-permute-done.27.r3
  145.5 1.0 copy-done.5
  146.5 1.0 copy-done.9
  147.5 1.0 copy-done.11
  148.6 0.7 copy-done.24
  149.3 2.1 %shard_map.112 = (f32[16,64,128]{2,1,0:T(8,128)}, f32[16,64,128]{2,1,0:T(8,128)}) custom-call(s32[93]{0:T(128)S(1)} %copy-done.24, f32[32,8,128]{2,1,0:T(8,128)S(1)} %all-to-all-done.1.sums_ref, f32[16,64,128]{2,1,0:T(8,128)S(1)} %get-tuple-element.81.v0, f32[16,64,128]{2,1,0:T(8,128)S(1)} %copy-done.5, f32[16,64,128]{2,1,0:T(8,128)S(1)} %copy-done.9, ...), custom_call_target="tpu_custom_call" | custom-call | tf_op jit(solution)/shard_map/pallas_call | solution.py:231
  (78 shorter events, 4.1 us)
Async XLA Ops:
  0.6 39.1 %copy-start.22 = (f32[16,128]{1,0:T(8,128)S(1)}, f32[16,128]{1,0:T(8,128)}, u32[]{:S(2)}) copy-start(f32[16,128]{1,0:T(8,128)} %diag_ref.11) | copy-start | bytes 24580
  2.2 1.4 copy-start.28
  4.3 1.0 copy-start.3
  5.3 22.9 %copy-start.25 = (s32[77]{0:T(128)}, s32[77]{0:T(128)S(1)}, u32[]{:S(2)}) copy-start(s32[77]{0:T(128)S(1)} %pad_add_fusion.1.meta_ref) | copy-start | bytes 928
  5.9 10.9 %collective-permute-start = (f32[2,64,128]{2,1,0:T(8,128)S(1)}, f32[2,64,128]{2,1,0:T(8,128)S(1)}, u32[]{:S(2)}, u32[]{:S(2)}) collective-permute-start(f32[2,64,128]{2,1,0:T(8,128)S(1)} %get-tuple-element.46), channel_id=1, source_target_pairs={{0,1},{1,2},{2,3},{3,4},{4,5},{5,6},{6,7},{7,8},{8,9},{9,10},{10,1... | collective-permute-start | bytes 196616 | tf_op jit(solution)/shard_map/ppermute | solution.py:269
  8.0 8.8 %collective-permute-start.1 = (f32[2,64,128]{2,1,0:T(8,128)S(1)}, f32[2,64,128]{2,1,0:T(8,128)S(1)}, u32[]{:S(2)}, u32[]{:S(2)}) collective-permute-start(f32[2,64,128]{2,1,0:T(8,128)S(1)} %get-tuple-element.47), channel_id=1, source_target_pairs={{0,31},{1,0},{2,1},{3,2},{4,3},{5,4},{6,5},{7,6},{8,7},{9,8},{10,9... | collective-permute-start | bytes 196616 | tf_op jit(solution)/shard_map/ppermute | solution.py:269
  14.6 3.5 %collective-permute-start.2 = (f32[2,64,128]{2,1,0:T(8,128)S(1)}, f32[2,64,128]{2,1,0:T(8,128)S(1)}, u32[]{:S(2)}, u32[]{:S(2)}) collective-permute-start(f32[2,64,128]{2,1,0:T(8,128)S(1)} %get-tuple-element.48), channel_id=1, source_target_pairs={{0,32},{32,64},{64,96},{96,128},{128,160},{160,192},{192,224},{224... | collective-permute-start | bytes 196616 | tf_op jit(solution)/shard_map/ppermute | solution.py:269
  16.8 3.7 %collective-permute-start.3 = (f32[2,64,128]{2,1,0:T(8,128)S(1)}, f32[2,64,128]{2,1,0:T(8,128)S(1)}, u32[]{:S(2)}, u32[]{:S(2)}) collective-permute-start(f32[2,64,128]{2,1,0:T(8,128)S(1)} %get-tuple-element.49), channel_id=1, source_target_pairs={{0,224},{32,0},{64,32},{96,64},{128,96},{160,128},{192,160},{224,1... | collective-permute-start | bytes 196616 | tf_op jit(solution)/shard_map/ppermute | solution.py:269
  20.5 2.2 %copy-start.1 = (f32[16,4,128,128]{3,2,1,0:T(8,128)S(1)}, f32[16,4,128,128]{3,2,1,0:T(8,128)}, u32[]{:S(2)}) copy-start(f32[16,4,128,128]{3,2,1,0:T(8,128)} %tile_ref.10) | copy-start | bytes 12582916
  22.7 0.7 copy-start.20
  23.4 38.0 %copy-start.21 = (f32[16,128]{1,0:T(8,128)S(1)}, f32[16,128]{1,0:T(8,128)}, u32[]{:S(2)}) copy-start(f32[16,128]{1,0:T(8,128)} %diag_ref.10) | copy-start | bytes 24580
  23.4 55.1 %slice-start = ((s8[5242880]{0:T(1024)(128)(4,1)}), s8[1048576]{0:T(1024)(128)(4,1)S(1)}, s32[]{:S(2)}) async-start(s8[5242880]{0:T(1024)(128)(4,1)} %bitcast.4), calls=%async_computation.2 | async-start | bytes 2097152
  28.2 9.5 %collective-permute-start.4 = (f32[4,64,128]{2,1,0:T(8,128)S(1)}, f32[4,64,128]{2,1,0:T(8,128)S(1)}, u32[]{:S(2)}, u32[]{:S(2)}) collective-permute-start(f32[4,64,128]{2,1,0:T(8,128)S(1)} %get-tuple-element.51.refs_1_), channel_id=1, source_target_pairs={{0,1},{1,2},{2,3},{3,4},{4,5},{5,6},{6,7},{7,8},{8,9},{9,10},{10,1... | collective-permute-start | bytes 393224 | tf_op jit(solution)/shard_map/ppermute | solution.py:269
  28.3 10.1 %collective-permute-start.5 = (f32[4,64,128]{2,1,0:T(8,128)S(1)}, f32[4,64,128]{2,1,0:T(8,128)S(1)}, u32[]{:S(2)}, u32[]{:S(2)}) collective-permute-start(f32[4,64,128]{2,1,0:T(8,128)S(1)} %get-tuple-element.52.refs_2_), channel_id=1, source_target_pairs={{0,31},{1,0},{2,1},{3,2},{4,3},{5,4},{6,5},{7,6},{8,7},{9,8},{10,9... | collective-permute-start | bytes 393224 | tf_op jit(solution)/shard_map/ppermute | solution.py:269
  33.1 6.0 %collective-permute-start.6 = (f32[4,64,128]{2,1,0:T(8,128)S(1)}, f32[4,64,128]{2,1,0:T(8,128)S(1)}, u32[]{:S(2)}, u32[]{:S(2)}) collective-permute-start(f32[4,64,128]{2,1,0:T(8,128)S(1)} %get-tuple-element.53.refs_3_), channel_id=1, source_target_pairs={{0,32},{32,64},{64,96},{96,128},{128,160},{160,192},{192,224},{224... | collective-permute-start | bytes 393224 | tf_op jit(solution)/shard_map/ppermute | solution.py:269
  33.6 6.0 %collective-permute-start.7 = (f32[4,64,128]{2,1,0:T(8,128)S(1)}, f32[4,64,128]{2,1,0:T(8,128)}, u32[]{:S(2)}, u32[]{:S(2)}) collective-permute-start(f32[4,64,128]{2,1,0:T(8,128)S(1)} %get-tuple-element.54.refs_4_), channel_id=1, source_target_pairs={{0,224},{32,0},{64,32},{96,64},{128,96},{160,128},{192,160},{224,1... | collective-permute-start | bytes 393224 | tf_op jit(solution)/shard_map/ppermute | solution.py:269
  33.7 0.7 copy-start.12
  37.0 24.3 %copy-start.26 = (s32[77]{0:T(128)S(1)}, s32[77]{0:T(128)}, u32[]{:S(2)}) copy-start(s32[77]{0:T(128)} %copy-done.25) | copy-start | bytes 928
  37.7 0.7 copy-start.14
  38.4 0.6 copy-start.16
  39.0 0.7 copy-start.18
  39.7 2.5 %copy-start = (f32[16,5,128,128]{3,2,1,0:T(8,128)S(1)}, f32[16,5,128,128]{3,2,1,0:T(8,128)}, u32[]{:S(2)}) copy-start(f32[16,5,128,128]{3,2,1,0:T(8,128)} %tile_ref.11) | copy-start | bytes 15728644
  42.2 0.9 copy-start.13
  43.1 0.9 copy-start.15
  44.0 0.9 copy-start.17
  44.9 0.9 copy-start.19
  45.8 32.7 %slice-start.1 = ((s8[5242880]{0:T(1024)(128)(4,1)}), s8[4194304]{0:T(1024)(128)(4,1)S(1)}, s32[]{:S(2)}) async-start(s8[5242880]{0:T(1024)(128)(4,1)} %bitcast.4), calls=%async_computation.3 | async-start | bytes 8388608
  49.8 8.4 %collective-permute-start.8 = (f32[4,64,128]{2,1,0:T(8,128)S(1)}, f32[4,64,128]{2,1,0:T(8,128)S(1)}, u32[]{:S(2)}, u32[]{:S(2)}) collective-permute-start(f32[4,64,128]{2,1,0:T(8,128)S(1)} %get-tuple-element.57.refs_1_), channel_id=1, source_target_pairs={{0,1},{1,2},{2,3},{3,4},{4,5},{5,6},{6,7},{7,8},{8,9},{9,10},{10,1... | collective-permute-start | bytes 393224 | tf_op jit(solution)/shard_map/ppermute | solution.py:269
  49.9 8.3 %collective-permute-start.9 = (f32[4,64,128]{2,1,0:T(8,128)S(1)}, f32[4,64,128]{2,1,0:T(8,128)S(1)}, u32[]{:S(2)}, u32[]{:S(2)}) collective-permute-start(f32[4,64,128]{2,1,0:T(8,128)S(1)} %get-tuple-element.58.refs_2_), channel_id=1, source_target_pairs={{0,31},{1,0},{2,1},{3,2},{4,3},{5,4},{6,5},{7,6},{8,7},{9,8},{10,9... | collective-permute-start | bytes 393224 | tf_op jit(solution)/shard_map/ppermute | solution.py:269
  54.6 4.4 %collective-permute-start.10 = (f32[4,64,128]{2,1,0:T(8,128)S(1)}, f32[4,64,128]{2,1,0:T(8,128)S(1)}, u32[]{:S(2)}, u32[]{:S(2)}) collective-permute-start(f32[4,64,128]{2,1,0:T(8,128)S(1)} %get-tuple-element.59.refs_3_), channel_id=1, source_target_pairs={{0,32},{32,64},{64,96},{96,128},{128,160},{160,192},{192,224},{224... | collective-permute-start | bytes 393224 | tf_op jit(solution)/shard_map/ppermute | solution.py:269
  56.9 4.4 %collective-permute-start.11 = (f32[4,64,128]{2,1,0:T(8,128)S(1)}, f32[4,64,128]{2,1,0:T(8,128)S(1)}, u32[]{:S(2)}, u32[]{:S(2)}) collective-permute-start(f32[4,64,128]{2,1,0:T(8,128)S(1)} %get-tuple-element.60.refs_4_), channel_id=1, source_target_pairs={{0,224},{32,0},{64,32},{96,64},{128,96},{160,128},{192,160},{224,1... | collective-permute-start | bytes 393224 | tf_op jit(solution)/shard_map/ppermute | solution.py:269
  61.3 2.2 %copy-start.2 = (f32[16,4,128,128]{3,2,1,0:T(8,128)S(1)}, f32[16,4,128,128]{3,2,1,0:T(8,128)}, u32[]{:S(2)}) copy-start(f32[16,4,128,128]{3,2,1,0:T(8,128)} %tile_ref.10) | copy-start | bytes 12582916
  68.4 7.9 %collective-permute-start.12 = (f32[4,64,128]{2,1,0:T(8,128)S(1)}, f32[4,64,128]{2,1,0:T(8,128)S(1)}, u32[]{:S(2)}, u32[]{:S(2)}) collective-permute-start(f32[4,64,128]{2,1,0:T(8,128)S(1)} %get-tuple-element.62.refs_1_), channel_id=1, source_target_pairs={{0,1},{1,2},{2,3},{3,4},{4,5},{5,6},{6,7},{7,8},{8,9},{9,10},{10,1... | collective-permute-start | bytes 393224 | tf_op jit(solution)/shard_map/ppermute | solution.py:269
  68.4 7.8 %collective-permute-start.13 = (f32[4,64,128]{2,1,0:T(8,128)S(1)}, f32[4,64,128]{2,1,0:T(8,128)S(1)}, u32[]{:S(2)}, u32[]{:S(2)}) collective-permute-start(f32[4,64,128]{2,1,0:T(8,128)S(1)} %get-tuple-element.63.refs_2_), channel_id=1, source_target_pairs={{0,31},{1,0},{2,1},{3,2},{4,3},{5,4},{6,5},{7,6},{8,7},{9,8},{10,9... | collective-permute-start | bytes 393224 | tf_op jit(solution)/shard_map/ppermute | solution.py:269
  73.2 3.9 %collective-permute-start.14 = (f32[4,64,128]{2,1,0:T(8,128)S(1)}, f32[4,64,128]{2,1,0:T(8,128)S(1)}, u32[]{:S(2)}, u32[]{:S(2)}) collective-permute-start(f32[4,64,128]{2,1,0:T(8,128)S(1)} %get-tuple-element.64.refs_3_), channel_id=1, source_target_pairs={{0,32},{32,64},{64,96},{96,128},{128,160},{160,192},{192,224},{224... | collective-permute-start | bytes 393224 | tf_op jit(solution)/shard_map/ppermute | solution.py:269
  73.8 4.7 %collective-permute-start.15 = (f32[4,64,128]{2,1,0:T(8,128)S(1)}, f32[4,64,128]{2,1,0:T(8,128)S(1)}, u32[]{:S(2)}, u32[]{:S(2)}) collective-permute-start(f32[4,64,128]{2,1,0:T(8,128)S(1)} %get-tuple-element.65.refs_4_), channel_id=1, source_target_pairs={{0,224},{32,0},{64,32},{96,64},{128,96},{160,128},{192,160},{224,1... | collective-permute-start | bytes 393224 | tf_op jit(solution)/shard_map/ppermute | solution.py:269
  81.8 0.8 copy-start.4
  82.6 8.7 %collective-permute-start.16 = (f32[4,64,128]{2,1,0:T(8,128)S(1)}, f32[4,64,128]{2,1,0:T(8,128)S(1)}, u32[]{:S(2)}, u32[]{:S(2)}) collective-permute-start(f32[4,64,128]{2,1,0:T(8,128)S(1)} %get-tuple-element.68.refs_1_), channel_id=1, source_target_pairs={{0,1},{1,2},{2,3},{3,4},{4,5},{5,6},{6,7},{7,8},{8,9},{9,10},{10,1... | collective-permute-start | bytes 393224 | tf_op jit(solution)/shard_map/ppermute | solution.py:269
  82.6 8.7 %collective-permute-start.17 = (f32[4,64,128]{2,1,0:T(8,128)S(1)}, f32[4,64,128]{2,1,0:T(8,128)S(1)}, u32[]{:S(2)}, u32[]{:S(2)}) collective-permute-start(f32[4,64,128]{2,1,0:T(8,128)S(1)} %get-tuple-element.69.refs_2_), channel_id=1, source_target_pairs={{0,31},{1,0},{2,1},{3,2},{4,3},{5,4},{6,5},{7,6},{8,7},{9,8},{10,9... | collective-permute-start | bytes 393224 | tf_op jit(solution)/shard_map/ppermute | solution.py:269
  87.4 4.8 %collective-permute-start.18 = (f32[4,64,128]{2,1,0:T(8,128)S(1)}, f32[4,64,128]{2,1,0:T(8,128)S(1)}, u32[]{:S(2)}, u32[]{:S(2)}) collective-permute-start(f32[4,64,128]{2,1,0:T(8,128)S(1)} %get-tuple-element.70.refs_3_), channel_id=1, source_target_pairs={{0,32},{32,64},{64,96},{96,128},{128,160},{160,192},{192,224},{224... | collective-permute-start | bytes 393224 | tf_op jit(solution)/shard_map/ppermute | solution.py:269
  87.7 4.7 %collective-permute-start.19 = (f32[4,64,128]{2,1,0:T(8,128)S(1)}, f32[4,64,128]{2,1,0:T(8,128)S(1)}, u32[]{:S(2)}, u32[]{:S(2)}) collective-permute-start(f32[4,64,128]{2,1,0:T(8,128)S(1)} %get-tuple-element.71.refs_4_), channel_id=1, source_target_pairs={{0,224},{32,0},{64,32},{96,64},{128,96},{160,128},{192,160},{224,1... | collective-permute-start | bytes 393224 | tf_op jit(solution)/shard_map/ppermute | solution.py:269
  97.2 10.4 %copy-start.6 = (f32[16,64,128]{2,1,0:T(8,128)}, f32[16,64,128]{2,1,0:T(8,128)S(1)}, u32[]{:S(2)}) copy-start(f32[16,64,128]{2,1,0:T(8,128)S(1)} %get-tuple-element.84.w2) | copy-start | bytes 1572868
  97.2 10.4 %collective-permute-start.20 = (f32[4,64,128]{2,1,0:T(8,128)S(1)}, f32[4,64,128]{2,1,0:T(8,128)S(1)}, u32[]{:S(2)}, u32[]{:S(2)}) collective-permute-start(f32[4,64,128]{2,1,0:T(8,128)S(1)} %get-tuple-element.73.refs_1_), channel_id=1, source_target_pairs={{0,1},{1,2},{2,3},{3,4},{4,5},{5,6},{6,7},{7,8},{8,9},{9,10},{10,1... | collective-permute-start | bytes 393224 | tf_op jit(solution)/shard_map/ppermute | solution.py:269
  97.3 10.3 %collective-permute-start.21 = (f32[4,64,128]{2,1,0:T(8,128)S(1)}, f32[4,64,128]{2,1,0:T(8,128)S(1)}, u32[]{:S(2)}, u32[]{:S(2)}) collective-permute-start(f32[4,64,128]{2,1,0:T(8,128)S(1)} %get-tuple-element.74.refs_2_), channel_id=1, source_target_pairs={{0,31},{1,0},{2,1},{3,2},{4,3},{5,4},{6,5},{7,6},{8,7},{9,8},{10,9... | collective-permute-start | bytes 393224 | tf_op jit(solution)/shard_map/ppermute | solution.py:269
  102.1 6.0 %collective-permute-start.22 = (f32[4,64,128]{2,1,0:T(8,128)S(1)}, f32[4,64,128]{2,1,0:T(8,128)S(1)}, u32[]{:S(2)}, u32[]{:S(2)}) collective-permute-start(f32[4,64,128]{2,1,0:T(8,128)S(1)} %get-tuple-element.75.refs_3_), channel_id=1, source_target_pairs={{0,32},{32,64},{64,96},{96,128},{128,160},{160,192},{192,224},{224... | collective-permute-start | bytes 393224 | tf_op jit(solution)/shard_map/ppermute | solution.py:269
  102.4 5.9 %collective-permute-start.23 = (f32[4,64,128]{2,1,0:T(8,128)S(1)}, f32[4,64,128]{2,1,0:T(8,128)S(1)}, u32[]{:S(2)}, u32[]{:S(2)}) collective-permute-start(f32[4,64,128]{2,1,0:T(8,128)S(1)} %get-tuple-element.76.refs_4_), channel_id=1, source_target_pairs={{0,224},{32,0},{64,32},{96,64},{128,96},{160,128},{192,160},{224,1... | collective-permute-start | bytes 393224 | tf_op jit(solution)/shard_map/ppermute | solution.py:269
  107.6 37.8 %copy-start.7 = (f32[16,64,128]{2,1,0:T(8,128)S(1)}, f32[16,64,128]{2,1,0:T(8,128)}, u32[]{:S(2)}) copy-start(f32[16,64,128]{2,1,0:T(8,128)} %copy-done.6) | copy-start | bytes 1572868
  111.5 0.8 copy-start.8
  112.3 0.8 copy-start.10
  113.1 0.6 copy-start.23
  113.7 0.7 copy-start.27
  128.4 17.1 %all-to-all-start.1 = ((f32[32,8,128]{2,1,0:T(8,128)}), f32[32,8,128]{2,1,0:T(8,128)S(1)}, u32[]{:S(2)}, u32[]{:S(2)}) async-start(f32[32,8,128]{2,1,0:T(8,128)} %broadcast_in_dim.2), calls=%async_computation.1 | async-start | bytes 262144 | tf_op jit(solution)/shard_map/all_to_all | solution.py:301
  134.2 10.2 %collective-permute-start.24 = (f32[4,64,128]{2,1,0:T(8,128)}, f32[4,64,128]{2,1,0:T(8,128)S(1)}, u32[]{:S(2)}, u32[]{:S(2)}) collective-permute-start(f32[4,64,128]{2,1,0:T(8,128)} %copy-done.27), channel_id=1, source_target_pairs={{0,1},{1,2},{2,3},{3,4},{4,5},{5,6},{6,7},{7,8},{8,9},{9,10},{10,1... | collective-permute-start | bytes 393224 | tf_op jit(solution)/shard_map/ppermute | solution.py:269
  135.5 8.9 %collective-permute-start.25 = (f32[4,64,128]{2,1,0:T(8,128)S(1)}, f32[4,64,128]{2,1,0:T(8,128)S(1)}, u32[]{:S(2)}, u32[]{:S(2)}) collective-permute-start(f32[4,64,128]{2,1,0:T(8,128)S(1)} %get-tuple-element.87), channel_id=1, source_target_pairs={{0,31},{1,0},{2,1},{3,2},{4,3},{5,4},{6,5},{7,6},{8,7},{9,8},{10,9... | collective-permute-start | bytes 393224 | tf_op jit(solution)/shard_map/ppermute | solution.py:269
  139.0 5.4 %collective-permute-start.26 = (f32[4,64,128]{2,1,0:T(8,128)S(1)}, f32[4,64,128]{2,1,0:T(8,128)S(1)}, u32[]{:S(2)}, u32[]{:S(2)}) collective-permute-start(f32[4,64,128]{2,1,0:T(8,128)S(1)} %get-tuple-element.88), channel_id=1, source_target_pairs={{0,32},{32,64},{64,96},{96,128},{128,160},{160,192},{192,224},{224... | collective-permute-start | bytes 393224 | tf_op jit(solution)/shard_map/ppermute | solution.py:269
  140.8 4.7 %collective-permute-start.27 = (f32[4,64,128]{2,1,0:T(8,128)S(1)}, f32[4,64,128]{2,1,0:T(8,128)S(1)}, u32[]{:S(2)}, u32[]{:S(2)}) collective-permute-start(f32[4,64,128]{2,1,0:T(8,128)S(1)} %get-tuple-element.89), channel_id=1, source_target_pairs={{0,224},{32,0},{64,32},{96,64},{128,96},{160,128},{192,160},{224,1... | collective-permute-start | bytes 393224 | tf_op jit(solution)/shard_map/ppermute | solution.py:269
  145.5 1.0 copy-start.5
  146.5 1.0 copy-start.9
  147.5 1.0 copy-start.11
  148.6 0.7 copy-start.24
